TPU v7x, 512 devices: a whole 4x8x8 slice. The times are simulated.
512 devices in a mesh: prow: 16 (over y, core), pcol: 32 (over x, z).
Axes of the slice: x: 4, y: 8, z: 8, core: 2. Of those that a mesh axis runs over, the one named last changes fastest.
Arguments:
- trailing: float32 [8, 16, 128, 4, 32, 128], P(None, 'prow', None, None, 'pcol'), may hold values from -8 to 8, as said below
- reflectors: float32 [8, 16, 128, 256], P(None, 'prow', None, 'pcol'), may hold values from -0.3125 to 0.3125
- tfactor: float32 [256, 256], replicated, may hold values from -0.375 to 0.375
Outputs:
- updated: float32 [8, 16, 128, 4, 32, 128], P(None, 'prow', None, None, 'pcol')
Inputs may be any that keep to these rules, and one draw needn't show every extreme that they name: trailing is symmetric as a matrix of order 16384.
All inputs are finite; a program needn't handle non-finite values.
Results may differ from a plain program's by a relative error of at most 0.00011.
Values sent between devices are 32-bit elements; how exact they have to be, the bound alone decides.
A program may use at most 64 MiB of HBM per device.

v0:
```python
import jax
import jax.numpy as jnp
from jax import lax
from jax.sharding import PartitionSpec as P


def spread(block, axis, holder):
    block = jnp.where(lax.axis_index(axis) == holder, block, jnp.zeros_like(block))
    return lax.psum(block, axis)


def matmul(left, right):
    return jnp.dot(left, right, precision=lax.Precision.HIGHEST, preferred_element_type=jnp.float32)


def per_device(trailing, reflectors, tfactor):
    row_tiles = trailing.shape[0]
    tile_size = trailing.shape[2]
    col_tiles = trailing.shape[3]
    local_rows = row_tiles * tile_size
    local_cols = col_tiles * tile_size
    local_block = trailing.reshape(local_rows, local_cols)
    col_index = lax.axis_index("pcol")
    group_ratio = lax.axis_size("pcol") // lax.axis_size("prow")
    mirror_owner = col_index % lax.axis_size("prow")
    mirror_slot = col_index // lax.axis_size("prow")
    y_rows = lax.all_gather(reflectors, "pcol", axis=3, tiled=True).reshape(local_rows, -1)
    panel_width = y_rows.shape[1]

    def mirror_rows(values):
        blocks = values.reshape(col_tiles, group_ratio, tile_size, panel_width)
        return lax.dynamic_index_in_dim(blocks, mirror_slot, 1, keepdims=False)

    y_cols = spread(mirror_rows(y_rows), "prow", mirror_owner).reshape(local_cols, panel_width)
    partial_rows = matmul(local_block, y_cols)
    ay_rows = lax.psum(partial_rows, "pcol")
    w_first = matmul(ay_rows, tfactor)
    inner_sum = lax.psum(matmul(y_rows.T, w_first), "prow")
    correction = matmul(tfactor.T, inner_sum)
    w_rows = w_first - 0.5 * matmul(y_rows, correction)
    w_cols = spread(mirror_rows(w_rows), "prow", mirror_owner).reshape(local_cols, panel_width)
    result = local_block - matmul(y_rows, w_cols.T) - matmul(w_rows, y_cols.T)
    return result.reshape(trailing.shape)


def solution(mesh):
    return jax.shard_map(
        per_device,
        mesh=mesh,
        in_specs=(P(None, "prow", None, None, "pcol", None), P(None, "prow", None, "pcol"), P()),
        out_specs=P(None, "prow", None, None, "pcol", None),
        check_vma=False,
    )
```

profile of v0, /device:TPU:1, one launch (start us, length us, event | category | flops | bytes accessed | tf_op | source)
XLA Modules:
  0.0 630.7 jit_solution(16274861302676822734)
XLA Ops:
  6.5 0.0 copy-start
  6.5 0.0 copy-start.1
  6.5 0.0 all-gather.2.cloned.1.call-start
  6.5 1.5 copy.15
  8.1 0.0 all-gather.2.cloned.1.call-update
  8.1 0.0 all-reduce.5.cloned.1.call-start
  8.2 85.7 %all-gather.2.cloned.1.call-done = f32[8,1,128,256]{2,0,1,3:T(8,128)} async-done(((f32[8,1,128,8]{2,0,1,3:T(8,128)}), f32[8,1,128,256]{2,0,1,3:T(8,128)}) %all-gather.2.cloned.1.call-update) | async-done | bytes 1048592 | tf_op jit(solution)/shard_map/all_gather | solution.py:27
  93.8 1.7 constant_dynamic-slice_fusion
  95.5 0.5 copy.24
  96.0 0.8 broadcast_select_fusion
  96.9 0.0 all-reduce.5.cloned.1.call-update
  96.9 0.0 all-reduce.7.cloned.1.call-start
  96.9 116.4 %all-reduce.5.cloned.1.call-done = f32[512,256]{1,0:T(8,128)} async-done(((f32[512,256]{1,0:T(8,128)}), f32[512,256]{1,0:T(8,128)}) %all-reduce.5.cloned.1.call-update) | async-done | bytes 524304 | tf_op jit(solution)/shard_map/psum | solution.py:9
  213.4 0.0 copy-done.1
  213.4 0.0 copy-start.3
  213.4 5.6 convolution_bitcast_fusion
  219.0 0.0 all-reduce.7.cloned.1.call-update
  219.0 0.0 all-reduce.9.cloned.1.call-start
  219.0 0.0 copy-done.3
  219.1 0.4 copy.17
  219.4 156.9 %all-reduce.7.cloned.1.call-done = f32[1024,256]{0,1:T(8,128)} async-done(((f32[1024,256]{0,1:T(8,128)}), f32[1024,256]{0,1:T(8,128)}) %all-reduce.7.cloned.1.call-update) | async-done | bytes 1048592 | tf_op jit(solution)/shard_map/psum | solution.py:36
  376.3 0.0 copy-done
  376.3 3.0 fusion.4
  379.4 2.5 convolution_bitcast_fusion.1
  381.9 0.0 all-reduce.9.cloned.1.call-update
  381.9 0.2 all-reduce.11.cloned.1.call-start
  382.1 3.1 copy.29
  385.2 2.9 copy.23
  388.2 109.3 %all-reduce.9.cloned.1.call-done = f32[256,256]{0,1:T(8,128)} async-done(((f32[256,256]{0,1:T(8,128)}), f32[256,256]{0,1:T(8,128)}) %all-reduce.9.cloned.1.call-update) | async-done | bytes 262160 | tf_op jit(solution)/shard_map/psum | solution.py:38
  497.5 1.3 fusion.5
  498.9 1.0 fusion.3
  499.9 0.0 copy-start.2
  499.9 1.0 copy-done.2
  500.9 0.8 dynamic-slice_select_fusion
  501.7 0.0 all-reduce.11.cloned.1.call-update
  501.7 3.2 fusion.6
  504.9 112.6 %all-reduce.11.cloned.1.call-done = f32[512,256]{1,0:T(8,128)} async-done(((f32[512,256]{1,0:T(8,128)}), f32[512,256]{1,0:T(8,128)}) %all-reduce.11.cloned.1.call-update) | async-done | bytes 524304 | tf_op jit(solution)/shard_map/psum | solution.py:9
  617.5 3.8 fusion.1
  621.3 0.5 copy.26
  621.8 2.3 copy.20
Async XLA Ops:
  6.5 369.8 %copy-start = (f32[256,256]{1,0:T(8,128)S(1)}, f32[256,256]{1,0:T(8,128)}, u32[]{:S(2)}) copy-start(f32[256,256]{1,0:T(8,128)} %param.5) | copy-start | bytes 786436
  6.5 206.8 %copy-start.1 = (f32[8,1,128,4,1,128]{5,4,3,2,1,0:T(1,128)S(1)}, f32[8,1,128,4,1,128]{5,4,3,2,1,0:T(1,128)}, u32[]{:S(2)}) copy-start(f32[8,1,128,4,1,128]{5,4,3,2,1,0:T(1,128)} %param.3) | copy-start | bytes 6291460
  6.5 87.3 %all-gather.2.cloned.1.call-start = ((), (), s32[]{:S(2)}) async-start(), calls=%async_computation | async-start | bytes 1081344 | tf_op jit(solution)/shard_map/all_gather | solution.py:27
  8.1 205.3 %all-reduce.5.cloned.1.call-start = ((), (), s32[]{:S(2)}) async-start(), calls=%async_computation.1 | async-start | bytes 1048576 | tf_op jit(solution)/shard_map/psum | solution.py:9
  96.9 279.4 %all-reduce.7.cloned.1.call-start = ((), (), s32[]{:S(2)}) async-start(), calls=%async_computation.2 | async-start | bytes 2097152 | tf_op jit(solution)/shard_map/psum | solution.py:36
  213.4 5.7 copy-start.3
  219.0 278.5 %all-reduce.9.cloned.1.call-start = ((), (), s32[]{:S(2)}) async-start(), calls=%async_computation.3 | async-start | bytes 524288 | tf_op jit(solution)/shard_map/psum | solution.py:38
  381.9 235.6 %all-reduce.11.cloned.1.call-start = ((), (), s32[]{:S(2)}) async-start(), calls=%async_computation.4 | async-start | bytes 1048576 | tf_op jit(solution)/shard_map/psum | solution.py:9
  499.9 1.0 copy-start.2
Sparse Core Ops, SparseCore 0:
  10.5 83.2 all-gather.1
  97.0 116.3 all-reduce.4
  219.1 157.1 all-reduce.6
  382.0 115.4 all-reduce.8
  501.8 115.6 all-reduce.10
where the time goes:
time: 631 us
  waiting for transfers between devices  581 us (92%)
  matrix products  20.6 us (3%)
  local copies, waits for them, and re-layouts  13.9 us (2%)
  between operations  13.3 us (2%)
    psum x2, waiting for transfers between devices, spread(): return lax.psum(block, axis)  229 us
    psum x1, waiting for transfers between devices, per_device(): ay_rows = lax.psum(partial_rows, 'pcol')  157 us
    psum x1, waiting for transfers between devices, per_device(): inner_sum = lax.psum(matmul(y_rows.T, w_first), 'prow')  109 us
    all_gather x1, waiting for transfers between devices, per_device(): lax.all_gather(reflectors, 'pcol', axis=3, tiled=True)  85.7 us
    dot_general x7, matrix products, matmul(): jnp.dot(left, right, precision=lax.Precision.HIGHEST, preferred_element_t...  20.6 us
  transfers between devices with their start and end apart: 5, of which 5 were waited for; matrix products, arithmetic and copies ran while one was open for 2% of the time, Pallas kernels for 0%

commit v1 on v0

v1 whole, which is shorter than its diff:
```python
import types

import jax
import jax.numpy as jnp
from jax import lax
from jax.experimental import pallas as pl
from jax.experimental.pallas import tpu as pltpu
from jax.sharding import PartitionSpec as P

F32 = jnp.float32
BF16 = jnp.bfloat16
MESH = pl.DeviceIdType.MESH
NX, NY, NZ, NC = 4, 8, 8, 2
RING = (1, 7, 2, 6, 3, 5, 4)


def wrap(value, size):
    return lax.rem(value + 2 * size, size)


def device(x, y, z, c):
    return (y * NC + c, x * NZ + z)


def split(value):
    high = value.astype(BF16)
    return high, (value - high.astype(F32)).astype(BF16)


def dot3(left, right, dims=((1,), (0,))):
    def one(a, b):
        return lax.dot_general(a, b, (dims, ((), ())), preferred_element_type=F32)

    return one(left[0], right[0]) + (one(left[0], right[1]) + one(left[1], right[0]))


def copy_to(src, dst, send, recv, target):
    return pltpu.make_async_remote_copy(
        src_ref=src, dst_ref=dst, send_sem=send, recv_sem=recv, device_id=target, device_id_type=MESH
    )


def kernel(
    yt_hbm, a_hbm, t_hbm, o_hbm,
    a_f32, a_hi, a_lo, t_f32, out,
    yr, yt_hi, yt_lo, yr_hi, yr_lo, yc, zt_hi, zt_lo, zt_f32,
    q_all, q_in, q_sum, r_in, gc, gr,
    n_own, n_z, n_zsum, n_x, n_all,
    local, o_sem,
    yz_s, yz_r, yx_s, yx_r, yv_s, yv_r,
    gz_s, gz_r, gx_s, gx_r, gv_s, gv_r,
    c1_s, c1_r, c2_s, c2_r, c3_s, c3_r,
    q_s, q_r, r_s, r_r, p_s, p_r, cy_s, cy_r, cc_s, cc_r,
    nz_s, nz_r, nx_s, nx_r, ny_s, ny_r, nc_s, nc_r,
):
    row, col = lax.axis_index("prow"), lax.axis_index("pcol")
    y, c = lax.div(row, NC), lax.rem(row, NC)
    x, z = lax.div(col, NZ), lax.rem(col, NZ)
    other = 1 - c
    sends = []

    def send(src, dst, send_sem, recv_sem, target):
        copy = copy_to(src, dst, send_sem, recv_sem, target)
        copy.start()
        sends.append(copy)

    def arrived(dst, send_sem, recv_sem, target):
        copy_to(dst, dst, send_sem, recv_sem, target).wait_recv()

    at_z = lambda d: device(x, y, wrap(z + d, NZ), c)
    at_x = lambda d: device(wrap(x + d, NX), y, z, c)
    at_y = lambda d: device(x, wrap(y + d, NY), z, c)
    at_c = device(x, y, z, other)

    row_x, row_z = lax.div(y, 4), 2 * lax.rem(y, 4) + c
    col_y, col_c = lax.rem(x, 2) * 4 + lax.div(z, 2), lax.rem(z, 2)

    mirror_y = wrap(y + z - row_z + 4, NY)
    mirror_dx = [wrap(x - row_x - 2 * s, NX) for s in range(2)]
    mirror_to = [device(row_x + 2 * s, mirror_y, row_z, lax.rem(mirror_dx[s], 2)) for s in range(2)]
    from_z = wrap(z + y - col_y + 4, NZ)
    from_x = [wrap(x + c + 2 * m, NX) for m in range(2)]
    mirror_from = [device(from_x[m], col_y, from_z, col_c) for m in range(2)]
    piece_to = device(wrap(x + c, NX), col_y, from_z, col_c)
    src_c = wrap(x - row_x, 2)
    src_x = wrap(x - src_c, NX)
    piece_from = device(src_x, mirror_y, row_z, src_c)

    barrier = pltpu.get_barrier_semaphore()
    greeted = [at_z(d) for d in RING] + [at_y(d) for d in RING] + [at_x(d) for d in (1, 2, 3)] + [at_c]
    greeted += mirror_to + mirror_from + [piece_to, piece_from]
    for peer in greeted:
        pl.semaphore_signal(barrier, inc=1, device_id=peer, device_id_type=MESH)

    y_in = pltpu.make_async_copy(yt_hbm, yr.at[x, z], local.at[0])
    a_in = pltpu.make_async_copy(a_hbm, a_f32, local.at[1])
    t_in = pltpu.make_async_copy(t_hbm, t_f32, local.at[2])
    y_in.start()
    a_in.start()
    t_in.start()
    y_in.wait()
    pl.semaphore_wait(barrier, len(greeted))

    def gather_begin(buf, slot, sems):
        own = buf.at[slot(0, 0)]
        for way, dx in ((0, 1), (1, -1)):
            send(own, own, sems.xs.at[way, 0], sems.xr.at[way, 0], at_x(dx))
        for i, d in enumerate(RING):
            send(own, own, sems.zs.at[i], sems.zr.at[i], at_z(d))

    def gather_z(buf, slot, sems, i):
        d = RING[i]
        block = buf.at[slot(0, -d)]
        arrived(block, sems.zs.at[i], sems.zr.at[i], at_z(-d))
        for way, dx in ((0, 1), (1, -1)):
            send(block, block, sems.xs.at[way, i + 1], sems.xr.at[way, i + 1], at_x(dx))

    def gather_x(buf, slot, sems, i):
        d = (0,) + RING
        for way, dx in ((0, 1), (1, -1)):
            block = buf.at[slot(-dx, -d[i])]
            arrived(block, sems.xs.at[way, i], sems.xr.at[way, i], at_x(-dx))
            if i % 2 == way:
                send(block, block, sems.vs.at[i], sems.vr.at[i], at_x(dx))

    def gather_end(buf, slot, sems, i):
        d = (0,) + RING
        dx = 1 if i % 2 == 0 else -1
        block = buf.at[slot(2, -d[i])]
        arrived(block, sems.vs.at[i], sems.vr.at[i], at_x(-dx))

    y_sems = types.SimpleNamespace(zs=yz_s, zr=yz_r, xs=yx_s, xr=yx_r, vs=yv_s, vr=yv_r)
    g_sems = types.SimpleNamespace(zs=gz_s, zr=gz_r, xs=gx_s, xr=gx_r, vs=gv_s, vr=gv_r)

    def y_slot(dx, dz):
        return (wrap(x + dx, NX), wrap(z + dz, NZ))

    def g_slot(dx, dz):
        at = wrap(x + dx, NX)
        part = wrap(at - row_x, 2)
        return (2 * lax.div(wrap(at - part, NX), 2) + part, wrap(y + z + dz - row_z + 4, NY))

    gather_begin(yr, y_slot, y_sems)
    for s in range(2):
        m = lax.div(mirror_dx[s], 2)
        send(yr.at[x, z, :, s], yc.at[x, z], c1_s.at[s], c1_r.at[m], mirror_to[s])

    a_in.wait()
    for tile in range(8):
        for b in range(4):
            high, low = split(a_f32[pl.ds(tile * 512 + b, 128, stride=4), :])
            a_hi[tile * 128 : tile * 128 + 128, b * 128 : b * 128 + 128] = high
            a_lo[tile * 128 : tile * 128 + 128, b * 128 : b * 128 + 128] = low

    for i in range(7):
        gather_z(yr, y_slot, y_sems, i)
        if i >= 2:
            gather_x(yr, y_slot, y_sems, i - 2)
    for m in range(2):
        block = yc.at[from_x[m], from_z]
        arrived(block, c1_s.at[m], c1_r.at[m], mirror_from[m])
        for i, d in enumerate(RING):
            send(block, block, c2_s.at[m, i], c2_r.at[m, i], at_y(d))
    for i in range(5, 8):
        gather_x(yr, y_slot, y_sems, i)
    for i in range(8):
        gather_end(yr, y_slot, y_sems, i)

    for tile in range(8):
        high, low = split(yr[:, :, tile // 2, tile % 2].reshape(256, 128))
        yt_hi[:, tile * 128 : tile * 128 + 128] = high
        yt_lo[:, tile * 128 : tile * 128 + 128] = low
    for half in range(2):
        cols = slice(half * 256, half * 256 + 256)
        part = dot3((yt_hi[...], yt_lo[...]), (a_hi[:, cols], a_lo[:, cols]))
        for k in range(2):
            q_all[:, :, :, half * 2 + k] = part[:, k * 128 : k * 128 + 128].reshape(2, 8, 2, 8, 128)
    send(q_all.at[other], q_in, q_s.at[0], q_r.at[0], at_c)

    for m in range(2):
        for i, d in enumerate(RING):
            block = yc.at[from_x[m], wrap(from_z - d, NZ)]
            arrived(block, c2_s.at[m, i], c2_r.at[m, i], at_y(-d))
        send(yc.at[from_x[m]], yc.at[from_x[m]], c3_s.at[m], c3_r.at[m], at_c)

    arrived(q_in, q_s.at[0], q_r.at[0], at_c)
    for i, d in enumerate(RING):
        to = wrap(y + d, NY)
        q_sum[to] = q_all[c, to] + q_in[to]
        send(q_sum.at[to], r_in.at[i], r_s.at[i], r_r.at[i], at_y(d))
    q_sum[y] = q_all[c, y] + q_in[y]

    for m in range(2):
        block = yc.at[wrap(x + other + 2 * m, NX)]
        arrived(block, c3_s.at[m], c3_r.at[m], at_c)
    t_in.wait()
    for b in range(4):
        rhs = split(yc[:, :, b].reshape(256, 128))
        part = dot3(split(t_f32[...]), rhs)
        zt_f32[:, b * 128 : b * 128 + 128] = part
        high, low = split(part)
        zt_hi[:, b * 128 : b * 128 + 128] = high
        zt_lo[:, b * 128 : b * 128 + 128] = low
    for tile in range(8):
        high, low = split(yr[:, :, tile // 2, tile % 2].reshape(256, 128).T)
        yr_hi[tile * 128 : tile * 128 + 128, :] = high
        yr_lo[tile * 128 : tile * 128 + 128, :] = low

    total = q_sum[y]
    for i, d in enumerate(RING):
        arrived(r_in.at[i], r_s.at[i], r_r.at[i], at_y(-d))
        total = total + r_in[i]
    gc[c, y] = total

    own = gc.at[c, y]
    send(own, gr.at[2 * lax.div(x, 2) + c, y], p_s.at[0], p_r.at[0], piece_to)
    for i, d in enumerate(RING):
        send(own, own, cy_s.at[i], cy_r.at[i], at_y(d))
    part = jnp.zeros((16, 256), F32)
    for b in range(4):
        part = part + dot3(
            split(total[:, b].reshape(16, 128)), split(yc[:, :, b].reshape(256, 128)), ((1,), (1,))
        )
    n_own[...] = part
    for i, d in enumerate(RING):
        send(n_own, n_z.at[i], nz_s.at[i], nz_r.at[i], at_z(d))

    arrived(gr.at[g_slot(0, 0)], p_s.at[0], p_r.at[0], piece_from)
    gather_begin(gr, g_slot, g_sems)

    part = n_own[...]
    for i, d in enumerate(RING):
        arrived(n_z.at[i], nz_s.at[i], nz_r.at[i], at_z(-d))
        part = part + n_z[i]
    n_zsum[...] = part
    for i in range(3):
        send(n_zsum, n_x.at[i], nx_s.at[i], nx_r.at[i], at_x(i + 1))

    for i in range(4):
        gather_z(gr, g_slot, g_sems, i)
    for i in range(3):
        arrived(n_x.at[i], nx_s.at[i], nx_r.at[i], at_x(-i - 1))
    n_all[c, y] = (n_zsum[...] + n_x[0]) + (n_x[1] + n_x[2])
    for i, d in enumerate(RING):
        send(n_all.at[c, y], n_all.at[c, y], ny_s.at[i], ny_r.at[i], at_y(d))
    for i in range(4, 7):
        gather_z(gr, g_slot, g_sems, i)
        gather_x(gr, g_slot, g_sems, i - 4)
    for i, d in enumerate(RING):
        arrived(gc.at[c, wrap(y - d, NY)], cy_s.at[i], cy_r.at[i], at_y(-d))
    send(gc.at[c], gc.at[c], cc_s.at[0], cc_r.at[0], at_c)
    for i in range(3, 8):
        gather_x(gr, g_slot, g_sems, i)
    for i, d in enumerate(RING):
        arrived(n_all.at[c, wrap(y - d, NY)], ny_s.at[i], ny_r.at[i], at_y(-d))
    send(n_all.at[c], n_all.at[c], nc_s.at[0], nc_r.at[0], at_c)
    for i in range(8):
        gather_end(gr, g_slot, g_sems, i)
    arrived(gc.at[other], cc_s.at[0], cc_r.at[0], at_c)
    arrived(n_all.at[other], nc_s.at[0], nc_r.at[0], at_c)

    inner = split(n_all[...].reshape(256, 256))
    vt = []
    for half in range(2):
        cols = slice(half * 256, half * 256 + 256)
        mirrored = jnp.concatenate([gc[:, :, :, half * 2 + k].reshape(256, 128) for k in range(2)], axis=1)
        corrected = mirrored - dot3(inner, (zt_hi[:, cols], zt_lo[:, cols]))
        vt.append(dot3(split(t_f32[...]), split(corrected), ((0,), (0,))))
    right_hi, right_lo = split(jnp.concatenate(vt, axis=1))

    writes = []
    for tile in range(8):
        rows = slice(tile * 128, tile * 128 + 128)
        pair = slice(tile % 2 * 2, tile % 2 * 2 + 2)
        g_rows = split(gr[pair, :, :, tile // 2].reshape(256, 128).T)
        update = dot3((yr_hi[rows, :], yr_lo[rows, :]), (right_hi, right_lo))
        update = update + dot3(g_rows, (zt_hi[...], zt_lo[...]))
        for b in range(4):
            at = pl.ds(tile * 512 + b, 128, stride=4)
            out[at, :] = a_f32[at, :] - update[:, b * 128 : b * 128 + 128]
        piece = pl.ds(tile * 512, 512)
        write = pltpu.make_async_copy(out.at[piece], o_hbm.at[piece], o_sem.at[tile])
        write.start()
        writes.append(write)
    for copy in sends:
        copy.wait_send()
    for write in writes:
        write.wait()


def per_device(trailing, reflectors, tfactor):
    flat = trailing.reshape(4096, 128)
    yt = jnp.transpose(reflectors.reshape(4, 2, 128, 8), (0, 1, 3, 2))
    dma = lambda *shape: pltpu.SemaphoreType.DMA(shape)
    vmem = lambda *shape: pltpu.VMEM(shape, F32)
    half = lambda *shape: pltpu.VMEM(shape, BF16)
    result = pl.pallas_call(
        kernel,
        out_shape=jax.ShapeDtypeStruct((4096, 128), F32),
        in_specs=[pl.BlockSpec(memory_space=pl.ANY)] * 3,
        out_specs=pl.BlockSpec(memory_space=pl.ANY),
        scratch_shapes=[
            vmem(4096, 128), half(1024, 512), half(1024, 512), vmem(256, 256), vmem(4096, 128),
            vmem(4, 8, 4, 2, 8, 128), half(256, 1024), half(256, 1024), half(1024, 256), half(1024, 256),
            vmem(4, 8, 4, 8, 128), half(256, 512), half(256, 512), vmem(256, 512),
            vmem(2, 8, 2, 4, 8, 128), vmem(8, 2, 4, 8, 128), vmem(8, 2, 4, 8, 128), vmem(7, 2, 4, 8, 128),
            vmem(2, 8, 2, 4, 8, 128), vmem(4, 8, 2, 4, 8, 128),
            vmem(16, 256), vmem(7, 16, 256), vmem(16, 256), vmem(3, 16, 256), vmem(2, 8, 16, 256),
            dma(3), dma(8),
            dma(7), dma(7), dma(2, 8), dma(2, 8), dma(8), dma(8),
            dma(7), dma(7), dma(2, 8), dma(2, 8), dma(8), dma(8),
            dma(2), dma(2), dma(2, 7), dma(2, 7), dma(2), dma(2),
            dma(1), dma(1), dma(7), dma(7), dma(1), dma(1), dma(7), dma(7), dma(1), dma(1),
            dma(7), dma(7), dma(3), dma(3), dma(7), dma(7), dma(1), dma(1),
        ],
        compiler_params=pltpu.CompilerParams(
            collective_id=0, has_side_effects=True, vmem_limit_bytes=60 * 2**20
        ),
    )(yt, flat, tfactor)
    return result.reshape(trailing.shape)


def solution(mesh):
    return jax.shard_map(
        per_device,
        mesh=mesh,
        in_specs=(P(None, "prow", None, None, "pcol", None), P(None, "prow", None, "pcol"), P()),
        out_specs=P(None, "prow", None, None, "pcol", None),
        check_vma=False,
    )
```

time: 631 us -> 76.2 us (0.12)
  waiting for transfers between devices: 581 us -> 0 us
  Pallas kernels: 0 us -> 71.7 us
  matrix products: 20.6 us -> 0 us
  between operations: 13.3 us -> 0.01 us
  local copies, waits for them, and re-layouts: 13.9 us -> 4.35 us
    psum x4 -> x0, waiting for transfers between devices: 495 us -> none  [the longest x2 229 us: spread(): return lax.psum(block, axis)]
    all_gather x1 -> x0, waiting for transfers between devices: 85.7 us -> none  [per_device(): lax.all_gather(reflectors, 'pcol', axis=3, tiled=True)]
    pallas_call x0 -> x1, Pallas kernels: none -> 71.7 us  [per_device(): pl.pallas_call(kernel, out_shape=jax.ShapeDtypeStruct((4096, 128), F32),...]
    dot_general x7 -> x0, matrix products: 20.6 us -> none  [matmul(): jnp.dot(left, right, precision=lax.Precision.HIGHEST, preferred_element_t...]
  transfers between devices with their start and end apart: 5 -> 0, of which waited for: 5 -> 0; matrix products, arithmetic and copies ran while one was open for 2% -> 0% of each run, Pallas kernels for 0% -> 0%
where the time goes in v1:
time: 76.2 us; the launch traced here: 76 us
  Pallas kernels  71.7 us (94%)
  local copies, waits for them, and re-layouts  4.35 us (6%)
    pallas_call x1, Pallas kernels, per_device(): pl.pallas_call(kernel, out_shape=jax.ShapeDtypeStruct((4096, 128), F32),...  71.7 us
    unnamed x1, local copies, waits for them, and re-layouts  4.35 us

profile of v1, /device:TPU:1, one launch (start us, length us, event | category | flops | bytes accessed | tf_op | source)
XLA Modules:
  0.0 76.0 jit_solution(5557687328176959566)
XLA Ops:
  0.0 71.7 %shard_map.37 = f32[4096,128]{1,0:T(8,128)} custom-call(f32[4,2,8,128]{3,2,1,0:T(8,128)} %bitcast.9, f32[4096,128]{1,0:T(8,128)} %bitcast.8, f32[256,256]{1,0:T(8,128)} %t_hbm.1), custom_call_target="tpu_custom_call" | custom-call | tf_op jit(solution)/shard_map/pallas_call | solution.py:297
  71.7 4.3 %copy.6 = f32[8,1,128,4,1,128]{5,4,3,2,1,0:T(1,128)} copy(f32[8,1,128,4,1,128]{5,4,3,2,1,0:T(1,128)} %bitcast.7) | data formatting | bytes 4194304

commit v2 on v1

v2 whole, which is shorter than its diff:
```python
import types

import jax
import jax.numpy as jnp
from jax import lax
from jax.experimental import pallas as pl
from jax.experimental.pallas import tpu as pltpu
from jax.sharding import PartitionSpec as P

F32 = jnp.float32
BF16 = jnp.bfloat16
MESH = pl.DeviceIdType.MESH
NX, NY, NZ, NC = 4, 8, 8, 2
RING = (1, 7, 2, 6, 3, 5, 4)
ONWARD = {2: ((4, 1), (6, 2)), 3: ((5, -1),)}
RELAYED = 4
RELAY_AFTER = {2: (0,), 3: (1,), 5: (2,), 6: (3,)}


def wrap(value, size):
    return lax.rem(value + 2 * size, size)


def device(x, y, z, c):
    return (y * NC + c, x * NZ + z)


def split(value):
    high = value.astype(BF16)
    return high, (value - high.astype(F32)).astype(BF16)


def dot3(left, right, dims=((1,), (0,))):
    def one(a, b):
        return lax.dot_general(a, b, (dims, ((), ())), preferred_element_type=F32)

    return one(left[0], right[0]) + (one(left[0], right[1]) + one(left[1], right[0]))


def in_order(blocks):
    return jnp.concatenate([blocks[:, :, j].reshape(128, blocks.shape[-1]) for j in range(2)], axis=0)


def copy_to(src, dst, send, recv, target):
    return pltpu.make_async_remote_copy(
        src_ref=src, dst_ref=dst, send_sem=send, recv_sem=recv, device_id=target, device_id_type=MESH
    )


def kernel(
    yt_hbm, a_hbm, t_hbm, yr_hi_out, yr_lo_out, vt_hi_out, vt_lo_out, a_out,
    a_f32, a_hi, a_lo, t_f32,
    yr, yr_hi, yr_lo, yc, yc_hi, yc_lo, zt_hi, zt_lo, vt_hi, vt_lo,
    q_part, q_in, q_sum, r_in, gc, gr,
    n_own, n_z, n_zsum, n_x, n_all,
    local, o_sem,
    yz_s, yz_r, yx_s, yx_r, yv_s, yv_r,
    gz_s, gz_r, gx_s, gx_r, gv_s, gv_r,
    c1_s, c1_r, c2_s, c2_r, c3_s, c3_r,
    q_s, q_r, r_s, r_r, p_s, p_r, cy_s, cy_r, cc_s, cc_r,
    nz_s, nz_r, nx_s, nx_r, ny_s, ny_r, nc_s, nc_r,
):
    row, col = lax.axis_index("prow"), lax.axis_index("pcol")
    y, c = lax.div(row, NC), lax.rem(row, NC)
    x, z = lax.div(col, NZ), lax.rem(col, NZ)
    other = 1 - c
    sends, writes = [], []

    def send(src, dst, send_sem, recv_sem, target):
        copy = copy_to(src, dst, send_sem, recv_sem, target)
        copy.start()
        sends.append(copy)

    def arrived(dst, send_sem, recv_sem, target):
        copy_to(dst, dst, send_sem, recv_sem, target).wait_recv()

    def write(src, dst):
        copy = pltpu.make_async_copy(src, dst, o_sem.at[len(writes)])
        copy.start()
        writes.append(copy)

    at_z = lambda d: device(x, y, wrap(z + d, NZ), c)
    at_x = lambda d: device(wrap(x + d, NX), y, z, c)
    at_y = lambda d: device(x, wrap(y + d, NY), z, c)
    at_c = device(x, y, z, other)

    row_x, row_z = lax.div(y, 4), 2 * lax.rem(y, 4) + c
    col_y, col_c = lax.rem(x, 2) * 4 + lax.div(z, 2), lax.rem(z, 2)

    mirror_y = wrap(y + z - row_z + 4, NY)
    mirror_dx = [wrap(x - row_x - 2 * s, NX) for s in range(2)]
    mirror_to = [device(row_x + 2 * s, mirror_y, row_z, lax.rem(mirror_dx[s], 2)) for s in range(2)]
    from_z = wrap(z + y - col_y + 4, NZ)
    from_x = [wrap(x + c + 2 * m, NX) for m in range(2)]
    mirror_from = [device(from_x[m], col_y, from_z, col_c) for m in range(2)]
    piece_to = device(wrap(x + c, NX), col_y, from_z, col_c)
    src_c = wrap(x - row_x, 2)
    src_x = wrap(x - src_c, NX)
    piece_from = device(src_x, mirror_y, row_z, src_c)

    first = lax.rem(x + c, 2)
    kept = (first, 3 - first)
    given = (1 - first, 2 + first)
    j_first = lax.div(wrap(x + first, NX), 2)
    j_at = (j_first, 1 - j_first)

    y_in = pltpu.make_async_copy(yt_hbm, yr.at[x, z], local.at[0])
    a_in = pltpu.make_async_copy(a_hbm, a_f32, local.at[1])
    t_in = pltpu.make_async_copy(t_hbm, t_f32, local.at[2])
    y_in.start()
    barrier = pltpu.get_barrier_semaphore()
    greeted = [at_z(d) for d in RING] + [at_x(d) for d in (1, 2, 3)] + [at_y(d) for d in RING] + [at_c]
    greeted += mirror_to + mirror_from + [piece_to, piece_from]
    for peer in greeted:
        pl.semaphore_signal(barrier, inc=1, device_id=peer, device_id_type=MESH)

    a_in.start()
    t_in.start()
    y_in.wait()
    pl.semaphore_wait(barrier, len(greeted))

    def gather_begin(buf, slot, sems):
        own = buf.at[slot(0, 0)]
        for way, dx in ((0, 1), (1, -1)):
            send(own, own, sems.xs.at[way, 0], sems.xr.at[way, 0], at_x(dx))
        for i in range(4):
            send(own, own, sems.zs.at[i], sems.zr.at[i], at_z(RING[i]))

    def gather_z(buf, slot, sems, i):
        d = RING[i]
        block = buf.at[slot(0, -d)]
        arrived(block, sems.zs.at[i], sems.zr.at[i], at_z(-d))
        for k, dz in ONWARD.get(i, ()):
            send(block, block, sems.zs.at[k], sems.zr.at[k], at_z(dz))
        if i + 1 >= RELAYED:
            send(block, block, sems.vs.at[i + 1], sems.vr.at[i + 1], at_x(2))
        for way, dx in ((0, 1), (1, -1)):
            send(block, block, sems.xs.at[way, i + 1], sems.xr.at[way, i + 1], at_x(dx))

    def gather_x(buf, slot, sems, i, ways=(0, 1)):
        d = (0,) + RING
        for way in ways:
            dx = 1 - 2 * way
            block = buf.at[slot(-dx, -d[i])]
            arrived(block, sems.xs.at[way, i], sems.xr.at[way, i], at_x(-dx))
            if i < RELAYED and i % 2 == way:
                send(block, block, sems.vs.at[i], sems.vr.at[i], at_x(dx))

    def gather_end(buf, slot, sems, i):
        d = (0,) + RING
        dx = 2 if i >= RELAYED else 1 - 2 * (i % 2)
        block = buf.at[slot(2, -d[i])]
        arrived(block, sems.vs.at[i], sems.vr.at[i], at_x(-dx))

    y_sems = types.SimpleNamespace(zs=yz_s, zr=yz_r, xs=yx_s, xr=yx_r, vs=yv_s, vr=yv_r)
    g_sems = types.SimpleNamespace(zs=gz_s, zr=gz_r, xs=gx_s, xr=gx_r, vs=gv_s, vr=gv_r)

    def y_slot(dx, dz):
        return (wrap(x + dx, NX), wrap(z + dz, NZ))

    def g_slot(dx, dz):
        at = wrap(x + dx, NX)
        part = wrap(at - row_x, 2)
        return (lax.div(wrap(at - part, NX), 2), part, wrap(y + z + dz - row_z + 4, NY))

    def multiply(t, dx):
        block = yr.at[wrap(x + dx, NX)]
        parts = [split(block[:, tile // 2, tile % 2].reshape(64, 128)) for tile in range(8)]
        high = jnp.concatenate([part[0] for part in parts], axis=1)
        low = jnp.concatenate([part[1] for part in parts], axis=1)
        both = jnp.concatenate([high, low], axis=0)
        for half in range(2):
            cols = slice(half * 256, half * 256 + 256)
            part = jnp.dot(both, a_hi[:, cols], preferred_element_type=F32)
            part = part[:64] + (part[64:] + jnp.dot(high, a_lo[:, cols], preferred_element_type=F32))
            for k in range(2):
                q_part[t, :, half * 2 + k] = part[:, k * 128 : k * 128 + 128].reshape(8, 8, 128)

    def to_core(h):
        send(q_part.at[given[h]], q_in.at[h], q_s.at[h], q_r.at[h], at_c)

    def scatter(h):
        arrived(q_in.at[h], q_s.at[h], q_r.at[h], at_c)
        for i, d in enumerate(RING):
            to = wrap(y + d, NY)
            q_sum[h, to] = q_part[kept[h], to] + q_in[h, to]
            send(q_sum.at[h, to], r_in.at[h, i], r_s.at[h, i], r_r.at[h, i], at_y(d))

    def collect(h):
        total = q_part[kept[h], y] + q_in[h, y]
        for i, d in enumerate(RING):
            arrived(r_in.at[h, i], r_s.at[h, i], r_r.at[h, i], at_y(-d))
            total = total + r_in[h, i]
        gc[c, y, j_at[h]] = total
        own = gc.at[c, y, j_at[h]]
        send(own, gr.at[lax.div(x, 2), c, y, j_at[h]], p_s.at[h], p_r.at[j_at[h]], piece_to)

    def begin_inner(h):
        left = split(gc[c, y, j_at[h]])
        part = jnp.zeros((8, 256), F32)
        for b in range(4):
            cols = slice(b * 128, b * 128 + 128)
            part = part + dot3((left[0][b], left[1][b]), (yc_hi[:, cols], yc_lo[:, cols]), ((1,), (1,)))
        n_own[h] = part
        for i, d in enumerate(RING):
            send(n_own.at[h], n_z.at[h, i], nz_s.at[h, i], nz_r.at[h, i], at_z(d))

    gather_begin(yr, y_slot, y_sems)
    for s in range(2):
        m = lax.div(mirror_dx[s], 2)
        send(yr.at[x, z, :, s], yc.at[x, z], c1_s.at[s], c1_r.at[m], mirror_to[s])

    def split_a(tiles):
        for tile in tiles:
            for b in range(4):
                high, low = split(a_f32[pl.ds(tile * 512 + b, 128, stride=4), :])
                a_hi[tile * 128 : tile * 128 + 128, b * 128 : b * 128 + 128] = high
                a_lo[tile * 128 : tile * 128 + 128, b * 128 : b * 128 + 128] = low

    def mirror(m):
        block = yc.at[from_x[m], from_z]
        arrived(block, c1_s.at[m], c1_r.at[m], mirror_from[m])
        for i, d in enumerate(RING):
            send(block, block, c2_s.at[m, i], c2_r.at[m, i], at_y(d))

    a_in.wait()
    split_a(range(4))
    for i in range(7):
        gather_z(yr, y_slot, y_sems, i)
        for k in RELAY_AFTER.get(i, ()):
            gather_x(yr, y_slot, y_sems, k)
        if i in (2, 3):
            mirror(i - 2)
    split_a(range(4, 8))
    multiply(0, 0)
    for i in range(RELAYED, 8):
        gather_x(yr, y_slot, y_sems, i, (1,))
    multiply(1, 1)
    to_core(0)
    for i in range(RELAYED, 8):
        gather_x(yr, y_slot, y_sems, i, (0,))
    multiply(2, -1)
    scatter(0)
    for i in range(8):
        gather_end(yr, y_slot, y_sems, i)
    multiply(3, 2)
    to_core(1)
    scatter(1)
    collect(0)
    for m in range(2):
        for i, d in enumerate(RING):
            block = yc.at[from_x[m], wrap(from_z - d, NZ)]
            arrived(block, c2_s.at[m, i], c2_r.at[m, i], at_y(-d))
        send(yc.at[from_x[m]], yc.at[from_x[m]], c3_s.at[m], c3_r.at[m], at_c)
    collect(1)
    for m in range(2):
        block = yc.at[wrap(x + other + 2 * m, NX)]
        arrived(block, c3_s.at[m], c3_r.at[m], at_c)
    for b in range(4):
        high, low = split(yc[:, :, b].reshape(256, 128))
        yc_hi[:, b * 128 : b * 128 + 128] = high
        yc_lo[:, b * 128 : b * 128 + 128] = low
    begin_inner(0)
    begin_inner(1)

    t_in.wait()
    t_parts = split(t_f32[...])
    for half in range(2):
        cols = slice(half * 256, half * 256 + 256)
        high, low = split(dot3(t_parts, (yc_hi[:, cols], yc_lo[:, cols])))
        zt_hi[:, cols] = high
        zt_lo[:, cols] = low
    for tile in range(8):
        high, low = split(yr[:, :, tile // 2, tile % 2].reshape(256, 128).T)
        yr_hi[tile * 128 : tile * 128 + 128, :] = high
        yr_lo[tile * 128 : tile * 128 + 128, :] = low
    write(yr_hi, yr_hi_out)
    write(yr_lo, yr_lo_out)

    own = gc.at[c, y]
    for i, d in enumerate(RING):
        send(own, own, cy_s.at[i], cy_r.at[i], at_y(d))
    own_s, own_k, own_y = g_slot(0, 0)
    for j in range(2):
        arrived(gr.at[own_s, own_k, own_y, j], p_s.at[j], p_r.at[j], piece_from)
    gather_begin(gr, g_slot, g_sems)

    for h in range(2):
        j = j_at[h]
        part = n_own[h]
        for i, d in enumerate(RING):
            arrived(n_z.at[h, i], nz_s.at[h, i], nz_r.at[h, i], at_z(-d))
            part = part + n_z[h, i]
        n_zsum[j] = part
    for i in range(3):
        send(n_zsum, n_x.at[i], nx_s.at[i], nx_r.at[i], at_x(i + 1))

    def gather_g(i):
        gather_z(gr, g_slot, g_sems, i)
        for k in RELAY_AFTER.get(i, ()):
            gather_x(gr, g_slot, g_sems, k)

    for i in range(4):
        gather_g(i)
    for i in range(3):
        arrived(n_x.at[i], nx_s.at[i], nx_r.at[i], at_x(-i - 1))
    n_all[c, y] = (n_zsum[...] + n_x[0]) + (n_x[1] + n_x[2])
    own_n = n_all.at[c, y]
    for i, d in enumerate(RING):
        send(own_n, own_n, ny_s.at[i], ny_r.at[i], at_y(d))
    for i in range(4, 7):
        gather_g(i)

    def subtract(s):
        for b in range(4):
            rows = split(in_order(gr[s, :, :, :, b]).T)
            part = dot3(rows, (zt_hi[...], zt_lo[...]))
            for k in range(4):
                at = pl.ds((2 * b + s) * 512 + k, 128, stride=4)
                a_f32[at, :] = a_f32[at, :] - part[:, k * 128 : k * 128 + 128]

    for i, d in enumerate(RING):
        arrived(gc.at[c, wrap(y - d, NY)], cy_s.at[i], cy_r.at[i], at_y(-d))
    send(gc.at[c], gc.at[c], cc_s.at[0], cc_r.at[0], at_c)
    for i in range(RELAYED, 8):
        gather_x(gr, g_slot, g_sems, i)
    subtract(own_s)
    for i in range(8):
        gather_end(gr, g_slot, g_sems, i)
    for i, d in enumerate(RING):
        arrived(n_all.at[c, wrap(y - d, NY)], ny_s.at[i], ny_r.at[i], at_y(-d))
    send(n_all.at[c], n_all.at[c], nc_s.at[0], nc_r.at[0], at_c)
    subtract(1 - own_s)
    write(a_f32, a_out)
    arrived(gc.at[other], cc_s.at[0], cc_r.at[0], at_c)
    arrived(n_all.at[other], nc_s.at[0], nc_r.at[0], at_c)

    inner = split(in_order(n_all[...]))
    for half in range(2):
        cols = slice(half * 256, half * 256 + 256)
        mirrored = jnp.concatenate([in_order(gc[:, :, :, half * 2 + k]) for k in range(2)], axis=1)
        corrected = mirrored - dot3(inner, (zt_hi[:, cols], zt_lo[:, cols]))
        high, low = split(dot3(t_parts, split(corrected), ((0,), (0,))))
        vt_hi[:, cols] = high
        vt_lo[:, cols] = low
    write(vt_hi, vt_hi_out)
    write(vt_lo, vt_lo_out)
    for copy in sends:
        copy.wait_send()
    for copy in writes:
        copy.wait()


def update(a, yr_hi, yr_lo, vt_hi, vt_lo, out):
    for s in range(4):
        rows = slice(s * 128, s * 128 + 128)
        part = dot3((yr_hi[rows, :], yr_lo[rows, :]), (vt_hi[...], vt_lo[...]))
        for b in range(4):
            at = pl.ds(s * 512 + b, 128, stride=4)
            out[at, :] = a[at, :] - part[:, b * 128 : b * 128 + 128]


def per_device(trailing, reflectors, tfactor):
    flat = trailing.reshape(4096, 128)
    yt = jnp.transpose(reflectors.reshape(4, 2, 128, 8), (0, 1, 3, 2))
    dma = lambda *shape: pltpu.SemaphoreType.DMA(shape)
    vmem = lambda *shape: pltpu.VMEM(shape, F32)
    half = lambda *shape: pltpu.VMEM(shape, BF16)
    out16 = lambda *shape: jax.ShapeDtypeStruct(shape, BF16)
    yr_hi, yr_lo, vt_hi, vt_lo, rest = pl.pallas_call(
        kernel,
        out_shape=[out16(1024, 256)] * 2 + [out16(256, 512)] * 2 + [jax.ShapeDtypeStruct((4096, 128), F32)],
        in_specs=[pl.BlockSpec(memory_space=pl.ANY)] * 3,
        out_specs=[pl.BlockSpec(memory_space=pl.ANY)] * 5,
        scratch_shapes=[
            vmem(4096, 128), half(1024, 512), half(1024, 512), vmem(256, 256),
            vmem(4, 8, 4, 2, 8, 128), half(1024, 256), half(1024, 256),
            vmem(4, 8, 4, 8, 128), *[half(256, 512)] * 6,
            vmem(4, 8, 4, 8, 128), vmem(2, 8, 4, 8, 128), vmem(2, 8, 4, 8, 128), vmem(2, 7, 4, 8, 128),
            vmem(2, 8, 2, 4, 8, 128), vmem(2, 2, 8, 2, 4, 8, 128),
            vmem(2, 8, 256), vmem(2, 7, 8, 256), vmem(2, 8, 256), vmem(3, 2, 8, 256), vmem(2, 8, 2, 8, 256),
            dma(3), dma(5),
            dma(7), dma(7), dma(2, 8), dma(2, 8), dma(8), dma(8),
            dma(7), dma(7), dma(2, 8), dma(2, 8), dma(8), dma(8),
            dma(2), dma(2), dma(2, 7), dma(2, 7), dma(2), dma(2),
            dma(2), dma(2), dma(2, 7), dma(2, 7), dma(2), dma(2), dma(7), dma(7), dma(1), dma(1),
            dma(2, 7), dma(2, 7), dma(3), dma(3), dma(7), dma(7), dma(1), dma(1),
        ],
        compiler_params=pltpu.CompilerParams(
            collective_id=0, has_side_effects=True, vmem_limit_bytes=60 * 2**20
        ),
    )(yt, flat, tfactor)
    whole = pl.BlockSpec((256, 512), lambda b: (0, 0))
    rows = pl.BlockSpec((512, 256), lambda b: (b, 0))
    tiles = pl.BlockSpec((2048, 128), lambda b: (b, 0))
    result = pl.pallas_call(
        update,
        grid=(2,),
        out_shape=jax.ShapeDtypeStruct((4096, 128), F32),
        in_specs=[tiles, rows, rows, whole, whole],
        out_specs=tiles,
        compiler_params=pltpu.CompilerParams(vmem_limit_bytes=60 * 2**20),
    )(rest, yr_hi, yr_lo, vt_hi, vt_lo)
    return result.reshape(trailing.shape)


def solution(mesh):
    return jax.shard_map(
        per_device,
        mesh=mesh,
        in_specs=(P(None, "prow", None, None, "pcol", None), P(None, "prow", None, "pcol"), P()),
        out_specs=P(None, "prow", None, None, "pcol", None),
        check_vma=False,
    )
```

time: 76.2 us -> 71.7 us (0.941)
  local copies, waits for them, and re-layouts: 4.35 us -> 0 us
    unnamed x1 -> x0, local copies, waits for them, and re-layouts: 4.35 us -> none
    pallas_call x1 -> x2, Pallas kernels: 71.7 us -> 71.6 us  [the longest x1 67.8 us: per_device(): pl.pallas_call(kernel, out_shape=[out16(1024, 256)] * 2 + [out16(256, 512...]
where the time goes in v2:
time: 71.7 us; the launch traced here: 71.6 us
  Pallas kernels  71.6 us (100%)
    pallas_call x1, Pallas kernels, per_device(): pl.pallas_call(kernel, out_shape=[out16(1024, 256)] * 2 + [out16(256, 512...  67.8 us
    pallas_call x1, Pallas kernels, per_device(): pl.pallas_call(update, grid=(2,), out_shape=jax.ShapeDtypeStruct((4096, 1...  3.78 us

profile of v2, /device:TPU:1, one launch (start us, length us, event | category | flops | bytes accessed | tf_op | source)
XLA Modules:
  0.0 71.6 jit_solution(3902622967802055942)
XLA Ops:
  0.0 67.8 %shard_map.37 = (bf16[1024,256]{1,0:T(8,128)(2,1)}, bf16[1024,256]{1,0:T(8,128)(2,1)}, bf16[256,512]{1,0:T(8,128)(2,1)}, bf16[256,512]{1,0:T(8,128)(2,1)}, f32[4096,128]{1,0:T(8,128)}) custom-call(f32[4,2,8,128]{3,2,1,0:T(8,128)} %bitcast.8, f32[4096,128]{1,0:T(8,128)} %bitcast.7, f32[256,256]{1,0:T(8,128)} %t_hbm.1), custom_call_target="tpu_custom_call" | custom-call | tf_op jit(solution)/shard_map/pallas_call | solution.py:370
  67.8 3.8 %shard_map.38 = f32[4096,128]{1,0:T(8,128)} custom-call(f32[4096,128]{1,0:T(8,128)} %get-tuple-element.10.a, bf16[1024,256]{1,0:T(8,128)(2,1)} %get-tuple-element.11.yr_hi, bf16[1024,256]{1,0:T(8,128)(2,1)} %get-tuple-element.12.yr_lo, bf16[256,512]{1,0:T(8,128)(2,1)} %get-tuple-element.13.vt_hi, bf16[256,512]{1,0:T(8,128)(2,1)} %get-tuple-element.14.vt_lo), custom_call_target="tpu_custom_call" | custom-call | tf_op jit(solution)/shard_map/pallas_call | solution.py:396

commit v3 on v2

--- a/solution.py
+++ b/solution.py
@@ -70,6 +70,11 @@
         copy = copy_to(src, dst, send_sem, recv_sem, target)
         copy.start()
         sends.append(copy)
+
+    def drain(count):
+        for copy in sends[:count]:
+            copy.wait_send()
+        del sends[:count]
 
     def arrived(dst, send_sem, recv_sem, target):
         copy_to(dst, dst, send_sem, recv_sem, target).wait_recv()
@@ -245,6 +250,7 @@
         gather_end(yr, y_slot, y_sems, i)
     multiply(3, 2)
     to_core(1)
+    started = len(sends)
     scatter(1)
     collect(0)
     for m in range(2):
@@ -252,7 +258,6 @@
             block = yc.at[from_x[m], wrap(from_z - d, NZ)]
             arrived(block, c2_s.at[m, i], c2_r.at[m, i], at_y(-d))
         send(yc.at[from_x[m]], yc.at[from_x[m]], c3_s.at[m], c3_r.at[m], at_c)
-    collect(1)
     for m in range(2):
         block = yc.at[wrap(x + other + 2 * m, NX)]
         arrived(block, c3_s.at[m], c3_r.at[m], at_c)
@@ -261,6 +266,8 @@
         yc_hi[:, b * 128 : b * 128 + 128] = high
         yc_lo[:, b * 128 : b * 128 + 128] = low
     begin_inner(0)
+    drain(started)
+    collect(1)
     begin_inner(1)
 
     t_in.wait()
@@ -280,6 +287,7 @@
     own = gc.at[c, y]
     for i, d in enumerate(RING):
         send(own, own, cy_s.at[i], cy_r.at[i], at_y(d))
+    drain(len(sends) - 7)
     own_s, own_k, own_y = g_slot(0, 0)
     for j in range(2):
         arrived(gr.at[own_s, own_k, own_y, j], p_s.at[j], p_r.at[j], piece_from)
@@ -330,6 +338,7 @@
     for i, d in enumerate(RING):
         arrived(n_all.at[c, wrap(y - d, NY)], ny_s.at[i], ny_r.at[i], at_y(-d))
     send(n_all.at[c], n_all.at[c], nc_s.at[0], nc_r.at[0], at_c)
+    drain(len(sends) - 1)
     subtract(1 - own_s)
     write(a_f32, a_out)
     arrived(gc.at[other], cc_s.at[0], cc_r.at[0], at_c)
@@ -345,8 +354,7 @@
         vt_lo[:, cols] = low
     write(vt_hi, vt_hi_out)
     write(vt_lo, vt_lo_out)
-    for copy in sends:
-        copy.wait_send()
+    drain(len(sends))
     for copy in writes:
         copy.wait()
 
@@ -387,9 +395,9 @@
             dma(2, 7), dma(2, 7), dma(3), dma(3), dma(7), dma(7), dma(1), dma(1),
         ],
         compiler_params=pltpu.CompilerParams(
-            collective_id=0, has_side_effects=True, vmem_limit_bytes=60 * 2**20
+            collective_id=0, has_side_effects=True, vmem_limit_bytes=28 * 2**20
         ),
-    )(yt, flat, tfactor)
+    )(*[pltpu.with_memory_space_constraint(value, pltpu.HBM) for value in (yt, flat, tfactor)])
     whole = pl.BlockSpec((256, 512), lambda b: (0, 0))
     rows = pl.BlockSpec((512, 256), lambda b: (b, 0))
     tiles = pl.BlockSpec((2048, 128), lambda b: (b, 0))
@@ -399,7 +407,7 @@
         out_shape=jax.ShapeDtypeStruct((4096, 128), F32),
         in_specs=[tiles, rows, rows, whole, whole],
         out_specs=tiles,
-        compiler_params=pltpu.CompilerParams(vmem_limit_bytes=60 * 2**20),
+        compiler_params=pltpu.CompilerParams(vmem_limit_bytes=20 * 2**20),
     )(rest, yr_hi, yr_lo, vt_hi, vt_lo)
     return result.reshape(trailing.shape)
 

time: 71.7 us -> 69.3 us (0.967)
  Pallas kernels: 71.6 us -> 68.8 us
    pallas_call x1, Pallas kernels: 3.78 us -> 2.18 us  [per_device(): pl.pallas_call(update, grid=(2,), out_shape=jax.ShapeDtypeStruct((4096, 1...]
    pallas_call x1, Pallas kernels: 67.8 us -> 66.6 us  [per_device(): pl.pallas_call(kernel, out_shape=[out16(1024, 256)] * 2 + [out16(256, 512...]
where the time goes in v3:
time: 69.3 us; the launch traced here: 68.8 us
  Pallas kernels  68.8 us (99%)
    pallas_call x1, Pallas kernels, per_device(): pl.pallas_call(kernel, out_shape=[out16(1024, 256)] * 2 + [out16(256, 512...  66.6 us
    pallas_call x1, Pallas kernels, per_device(): pl.pallas_call(update, grid=(2,), out_shape=jax.ShapeDtypeStruct((4096, 1...  2.18 us

profile of v3, /device:TPU:1, one launch (start us, length us, event | category | flops | bytes accessed | tf_op | source)
XLA Modules:
  0.0 68.8 jit_solution(4657513019452348710)
XLA Ops:
  0.0 66.6 %shard_map.37 = (bf16[1024,256]{1,0:T(8,128)(2,1)S(1)}, bf16[1024,256]{1,0:T(8,128)(2,1)S(1)}, bf16[256,512]{1,0:T(8,128)(2,1)S(1)}, bf16[256,512]{1,0:T(8,128)(2,1)S(1)}, f32[4096,128]{1,0:T(8,128)S(1)}) custom-call(f32[4,2,8,128]{3,2,1,0:T(8,128)} %bitcast.8, f32[4096,128]{1,0:T(8,128)} %bitcast.7, f32[256,256]{1,0:T(8,128)} %t_hbm.1), custom_call_target="tpu_custom_call" | custom-call | tf_op jit(solution)/shard_map/pallas_call | solution.py:378
  66.6 2.2 %shard_map.38 = f32[4096,128]{1,0:T(8,128)} custom-call(f32[4096,128]{1,0:T(8,128)S(1)} %get-tuple-element.10.a, bf16[1024,256]{1,0:T(8,128)(2,1)S(1)} %get-tuple-element.11.yr_hi, bf16[1024,256]{1,0:T(8,128)(2,1)S(1)} %get-tuple-element.12.yr_lo, bf16[256,512]{1,0:T(8,128)(2,1)S(1)} %get-tuple-element.13.vt_hi, bf16[256,512]{1,0:T(8,128)(2,1)S(1)} %get-tuple-element.14.vt_lo), custom_call_target="tpu_custom_call" | custom-call | tf_op jit(solution)/shard_map/pallas_call | solution.py:404

commit v4 on v3

--- a/solution.py
+++ b/solution.py
@@ -52,13 +52,13 @@
     a_f32, a_hi, a_lo, t_f32,
     yr, yr_hi, yr_lo, yc, yc_hi, yc_lo, zt_hi, zt_lo, vt_hi, vt_lo,
     q_part, q_in, q_sum, r_in, gc, gr,
-    n_own, n_z, n_zsum, n_x, n_all,
+    n_own, n_z, n_zsum, n_x,
     local, o_sem,
     yz_s, yz_r, yx_s, yx_r, yv_s, yv_r,
     gz_s, gz_r, gx_s, gx_r, gv_s, gv_r,
     c1_s, c1_r, c2_s, c2_r, c3_s, c3_r,
     q_s, q_r, r_s, r_r, p_s, p_r, cy_s, cy_r, cc_s, cc_r,
-    nz_s, nz_r, nx_s, nx_r, ny_s, ny_r, nc_s, nc_r,
+    nz_s, nz_r, nx_s, nx_r,
 ):
     row, col = lax.axis_index("prow"), lax.axis_index("pcol")
     y, c = lax.div(row, NC), lax.rem(row, NC)
@@ -284,10 +284,7 @@
     write(yr_hi, yr_hi_out)
     write(yr_lo, yr_lo_out)
 
-    own = gc.at[c, y]
-    for i, d in enumerate(RING):
-        send(own, own, cy_s.at[i], cy_r.at[i], at_y(d))
-    drain(len(sends) - 7)
+    drain(len(sends))
     own_s, own_k, own_y = g_slot(0, 0)
     for j in range(2):
         arrived(gr.at[own_s, own_k, own_y, j], p_s.at[j], p_r.at[j], piece_from)
@@ -312,10 +309,13 @@
         gather_g(i)
     for i in range(3):
         arrived(n_x.at[i], nx_s.at[i], nx_r.at[i], at_x(-i - 1))
-    n_all[c, y] = (n_zsum[...] + n_x[0]) + (n_x[1] + n_x[2])
-    own_n = n_all.at[c, y]
+    inner = split(((n_zsum[...] + n_x[0]) + (n_x[1] + n_x[2])).reshape(16, 256))
+    inner = dot3(inner, (zt_hi[...], zt_lo[...]))
+    for b in range(4):
+        gc[c, y, :, b] = gc[c, y, :, b] - inner[:, b * 128 : b * 128 + 128].reshape(2, 8, 128)
+    own = gc.at[c, y]
     for i, d in enumerate(RING):
-        send(own_n, own_n, ny_s.at[i], ny_r.at[i], at_y(d))
+        send(own, own, cy_s.at[i], cy_r.at[i], at_y(d))
     for i in range(4, 7):
         gather_g(i)
 
@@ -327,28 +327,20 @@
                 at = pl.ds((2 * b + s) * 512 + k, 128, stride=4)
                 a_f32[at, :] = a_f32[at, :] - part[:, k * 128 : k * 128 + 128]
 
+    for i in range(RELAYED, 8):
+        gather_x(gr, g_slot, g_sems, i)
+    subtract(own_s)
     for i, d in enumerate(RING):
         arrived(gc.at[c, wrap(y - d, NY)], cy_s.at[i], cy_r.at[i], at_y(-d))
     send(gc.at[c], gc.at[c], cc_s.at[0], cc_r.at[0], at_c)
-    for i in range(RELAYED, 8):
-        gather_x(gr, g_slot, g_sems, i)
-    subtract(own_s)
     for i in range(8):
         gather_end(gr, g_slot, g_sems, i)
-    for i, d in enumerate(RING):
-        arrived(n_all.at[c, wrap(y - d, NY)], ny_s.at[i], ny_r.at[i], at_y(-d))
-    send(n_all.at[c], n_all.at[c], nc_s.at[0], nc_r.at[0], at_c)
-    drain(len(sends) - 1)
     subtract(1 - own_s)
     write(a_f32, a_out)
     arrived(gc.at[other], cc_s.at[0], cc_r.at[0], at_c)
-    arrived(n_all.at[other], nc_s.at[0], nc_r.at[0], at_c)
-
-    inner = split(in_order(n_all[...]))
     for half in range(2):
         cols = slice(half * 256, half * 256 + 256)
-        mirrored = jnp.concatenate([in_order(gc[:, :, :, half * 2 + k]) for k in range(2)], axis=1)
-        corrected = mirrored - dot3(inner, (zt_hi[:, cols], zt_lo[:, cols]))
+        corrected = jnp.concatenate([in_order(gc[:, :, :, half * 2 + k]) for k in range(2)], axis=1)
         high, low = split(dot3(t_parts, split(corrected), ((0,), (0,))))
         vt_hi[:, cols] = high
         vt_lo[:, cols] = low
@@ -386,13 +378,13 @@
             vmem(4, 8, 4, 8, 128), *[half(256, 512)] * 6,
             vmem(4, 8, 4, 8, 128), vmem(2, 8, 4, 8, 128), vmem(2, 8, 4, 8, 128), vmem(2, 7, 4, 8, 128),
             vmem(2, 8, 2, 4, 8, 128), vmem(2, 2, 8, 2, 4, 8, 128),
-            vmem(2, 8, 256), vmem(2, 7, 8, 256), vmem(2, 8, 256), vmem(3, 2, 8, 256), vmem(2, 8, 2, 8, 256),
+            vmem(2, 8, 256), vmem(2, 7, 8, 256), vmem(2, 8, 256), vmem(3, 2, 8, 256),
             dma(3), dma(5),
             dma(7), dma(7), dma(2, 8), dma(2, 8), dma(8), dma(8),
             dma(7), dma(7), dma(2, 8), dma(2, 8), dma(8), dma(8),
             dma(2), dma(2), dma(2, 7), dma(2, 7), dma(2), dma(2),
             dma(2), dma(2), dma(2, 7), dma(2, 7), dma(2), dma(2), dma(7), dma(7), dma(1), dma(1),
-            dma(2, 7), dma(2, 7), dma(3), dma(3), dma(7), dma(7), dma(1), dma(1),
+            dma(2, 7), dma(2, 7), dma(3), dma(3),
         ],
         compiler_params=pltpu.CompilerParams(
             collective_id=0, has_side_effects=True, vmem_limit_bytes=28 * 2**20

time: 69.3 us -> 69.3 us (level)
  no operation moved by 1% of the time
where the time goes in v4:
time: 69.3 us; the launch traced here: 69 us
  Pallas kernels  69 us (100%)
    pallas_call x1, Pallas kernels, per_device(): pl.pallas_call(kernel, out_shape=[out16(1024, 256)] * 2 + [out16(256, 512...  66.9 us
    pallas_call x1, Pallas kernels, per_device(): pl.pallas_call(update, grid=(2,), out_shape=jax.ShapeDtypeStruct((4096, 1...  2.17 us

profile of v4, /device:TPU:1, one launch (start us, length us, event | category | flops | bytes accessed | tf_op | source)
XLA Modules:
  0.0 69.0 jit_solution(278030349679545397)
XLA Ops:
  0.0 66.9 %shard_map.37 = (bf16[1024,256]{1,0:T(8,128)(2,1)S(1)}, bf16[1024,256]{1,0:T(8,128)(2,1)S(1)}, bf16[256,512]{1,0:T(8,128)(2,1)S(1)}, bf16[256,512]{1,0:T(8,128)(2,1)S(1)}, f32[4096,128]{1,0:T(8,128)S(1)}) custom-call(f32[4,2,8,128]{3,2,1,0:T(8,128)} %bitcast.8, f32[4096,128]{1,0:T(8,128)} %bitcast.7, f32[256,256]{1,0:T(8,128)} %t_hbm.1), custom_call_target="tpu_custom_call" | custom-call | tf_op jit(solution)/shard_map/pallas_call | solution.py:370
  66.9 2.2 %shard_map.38 = f32[4096,128]{1,0:T(8,128)} custom-call(f32[4096,128]{1,0:T(8,128)S(1)} %get-tuple-element.10.a, bf16[1024,256]{1,0:T(8,128)(2,1)S(1)} %get-tuple-element.11.yr_hi, bf16[1024,256]{1,0:T(8,128)(2,1)S(1)} %get-tuple-element.12.yr_lo, bf16[256,512]{1,0:T(8,128)(2,1)S(1)} %get-tuple-element.13.vt_hi, bf16[256,512]{1,0:T(8,128)(2,1)S(1)} %get-tuple-element.14.vt_lo), custom_call_target="tpu_custom_call" | custom-call | tf_op jit(solution)/shard_map/pallas_call | solution.py:396
